TPU v7x, 32 devices: a whole 2x2x4 slice. The times are simulated.
32 devices in a mesh: dp: 8 (over z, x), tensor: 4 (over y, core).
Axes of the slice: x: 2, y: 2, z: 4, core: 2. Of those that a mesh axis runs over, the one named last changes fastest.
Arguments:
- layer_input: bfloat16 [4096, 768], P('dp', 'tensor'), may hold values from -6 to 6
- segment_ids: int32 [8, 512], P('dp'), may hold values from 0 to 15, never falling along the last dimension, each value on 1 to 256 neighbouring positions
- triple_weight: bfloat16 [768, 3, 768], P(None, None, 'tensor'), may hold values from -0.21875 to 0.21875
- query_value_bias: float32 [2, 768], P(None, 'tensor'), may hold values from -3 to 3
- output_weight: bfloat16 [768, 768], P('tensor'), may hold values from -0.875 to 0.875
- output_bias: float32 [768], P('tensor'), may hold values from -3 to 3
- norm_gain: float32 [768], P('tensor'), may hold values from 0.5 to 1.5
- norm_shift: float32 [768], P('tensor'), may hold values from -3 to 3
- expand_weight: bfloat16 [768, 3072], P(None, 'tensor'), may hold values from -0.21875 to 0.21875
- expand_bias: float32 [3072], P('tensor'), may hold values from -3 to 3
- reduce_weight: bfloat16 [3072, 768], P('tensor'), may hold values from -0.109375 to 0.109375
- reduce_bias: float32 [768], P('tensor'), may hold values from -3 to 3
- final_gain: float32 [768], P('tensor'), may hold values from 0.5 to 1.5
- final_shift: float32 [768], P('tensor'), may hold values from -3 to 3
- cotangent: bfloat16 [4096, 768], P('dp', 'tensor'), may hold values from -6 to 6
Outputs:
- layer_output: bfloat16 [4096, 768], P('dp', 'tensor')
- input_grad: float32 [4096, 768], P('dp', 'tensor')
- triple_grad: float32 [768, 3, 768], P(None, None, 'tensor')
- query_value_grad: float32 [2, 768], P(None, 'tensor')
- output_weight_grad: float32 [768, 768], P('tensor')
- output_bias_grad: float32 [768], P('tensor')
- norm_gain_grad: float32 [768], P('tensor')
- norm_shift_grad: float32 [768], P('tensor')
- expand_weight_grad: float32 [768, 3072], P(None, 'tensor')
- expand_bias_grad: float32 [3072], P('tensor')
- reduce_weight_grad: float32 [3072, 768], P('tensor')
- reduce_bias_grad: float32 [768], P('tensor')
- final_gain_grad: float32 [768], P('tensor')
- final_shift_grad: float32 [768], P('tensor')
Inputs may be any that keep to these rules, and one draw needn't show every extreme that they name: `segment_ids`: segment numbers never fall along a sequence; each document holds 1 to 256 tokens.
All inputs are finite; a program needn't handle non-finite values.
Results may differ from a plain program's by a relative error of at most 0.012.
The roundings to bfloat16 on the way count: a program that leaves them out, or rounds other values in their place, can miss the bound.
Values may be sent and summed in bfloat16 or wider, within the bound.
A program may use at most 64 MiB of HBM per device.

v0:
```python
import jax
import jax.numpy as jnp
from jax import lax
from jax.sharding import PartitionSpec as P

D = 768
HD = 64
EPS = 1e-06


def gelu_value(pre_act):
    return 0.5 * pre_act * (1.0 + lax.erf(pre_act * 0.7071067811865476))


def gelu_slope(pre_act):
    return (
        0.5 * (1.0 + lax.erf(pre_act * 0.7071067811865476))
        + pre_act * jnp.exp(-0.5 * pre_act * pre_act) * 0.3989422804014327
    )


def widen(piece):
    return lax.all_gather(piece, "tensor", axis=1, tiled=True)


def row_stats(first, second):
    return lax.psum((jnp.sum(first, axis=1), jnp.sum(second, axis=1)), "tensor")


def norm_forward(hidden, gain, shift):
    total, squares = row_stats(hidden, hidden * hidden)
    row_mean = (total / D)[:, None]
    inverse = lax.rsqrt(squares[:, None] / D - row_mean * row_mean + EPS)
    normed = (hidden - row_mean) * inverse
    return (normed * gain + shift, normed, inverse)


def norm_backward(upstream, normed, inverse, gain):
    scaled = upstream * gain
    first_total, second_total = row_stats(scaled, scaled * normed)
    return inverse * (scaled - first_total[:, None] / D - normed * second_total[:, None] / D)


def tall_dot(left, right):
    return lax.dot_general(
        left, right, (((0,), (0,)), ((), ())), preferred_element_type=jnp.float32
    )


def wide_dot(left, right):
    return lax.dot_general(
        left, right, (((1,), (1,)), ((), ())), preferred_element_type=jnp.float32
    )


def masked_scores(query_part, key_part, segment_row, head_scale):
    scores = (
        jnp.einsum("qhd,khd->hqk", query_part, key_part, preferred_element_type=jnp.float32)
        * head_scale
    )
    allowed = segment_row[:, None] == segment_row[None, :]
    return jnp.where(allowed[None], scores, -jnp.inf)


def per_device(
    layer_input,
    segment_ids,
    triple_weight,
    query_value_bias,
    output_weight,
    output_bias,
    norm_gain,
    norm_shift,
    expand_weight,
    expand_bias,
    reduce_weight,
    reduce_bias,
    final_gain,
    final_shift,
    cotangent,
):
    seq_count = segment_ids.shape[0]
    seq_len = segment_ids.shape[1]
    tok_count = seq_count * seq_len
    local_width = triple_weight.shape[2]
    local_heads = local_width // HD
    head_scale = HD ** (-0.5)
    gathered = widen(layer_input)
    projected = jnp.einsum(
        "td,dcf->tcf", gathered, triple_weight, preferred_element_type=jnp.float32
    )
    query_half = (
        (projected[:, 0] + query_value_bias[0])
        .astype(jnp.bfloat16)
        .reshape(seq_count, seq_len, local_heads, HD)
    )
    key_half = projected[:, 1].astype(jnp.bfloat16).reshape(seq_count, seq_len, local_heads, HD)
    value_half = (
        (projected[:, 2] + query_value_bias[1])
        .astype(jnp.bfloat16)
        .reshape(seq_count, seq_len, local_heads, HD)
    )
    seq_index = 0
    scores = masked_scores(
        query_half[seq_index], key_half[seq_index], segment_ids[seq_index], head_scale
    )
    top = jnp.max(scores, axis=-1, keepdims=True)
    log_total = top + jnp.log(jnp.sum(jnp.exp(scores - top), axis=-1, keepdims=True))
    probs_half = jnp.exp(scores - log_total).astype(jnp.bfloat16)
    context_list = [
        jnp.einsum(
            "hqk,khd->qhd", probs_half, value_half[seq_index], preferred_element_type=jnp.float32
        ).astype(jnp.bfloat16)
    ]
    total_list = [log_total]
    context = jnp.stack(context_list)
    context_flat = context.reshape(tok_count, local_width)
    attn_share = lax.psum_scatter(
        jnp.dot(context_flat, output_weight, preferred_element_type=jnp.float32),
        "tensor",
        scatter_dimension=1,
        tiled=True,
    )
    first_sum = layer_input.astype(jnp.float32) + attn_share + output_bias
    attended, normed_one, inv_one = norm_forward(first_sum, norm_gain, norm_shift)
    attended_half = widen(attended.astype(jnp.bfloat16))
    pre_act = (
        jnp.dot(attended_half, expand_weight, preferred_element_type=jnp.float32) + expand_bias
    )
    activated = gelu_value(pre_act).astype(jnp.bfloat16)
    mlp_share = lax.psum_scatter(
        jnp.dot(activated, reduce_weight, preferred_element_type=jnp.float32),
        "tensor",
        scatter_dimension=1,
        tiled=True,
    )
    second_sum = attended + mlp_share + reduce_bias
    out_f, normed_two, inv_two = norm_forward(second_sum, final_gain, final_shift)
    layer_output = out_f.astype(jnp.bfloat16)
    upstream = cotangent.astype(jnp.float32)
    final_gain_grad = jnp.sum(upstream * normed_two, axis=0)
    final_shift_grad = jnp.sum(upstream, axis=0)
    second_grad = norm_backward(upstream, normed_two, inv_two, final_gain)
    second_half = widen(second_grad.astype(jnp.bfloat16))
    reduce_weight_grad = tall_dot(activated, second_half)
    reduce_bias_grad = jnp.sum(second_grad, axis=0)
    act_grad = wide_dot(second_half, reduce_weight) * gelu_slope(pre_act)
    act_half = act_grad.astype(jnp.bfloat16)
    expand_weight_grad = tall_dot(attended_half, act_half)
    expand_bias_grad = jnp.sum(act_grad, axis=0)
    attended_grad = second_grad + lax.psum_scatter(
        wide_dot(act_half, expand_weight), "tensor", scatter_dimension=1, tiled=True
    )
    norm_gain_grad = jnp.sum(attended_grad * normed_one, axis=0)
    norm_shift_grad = jnp.sum(attended_grad, axis=0)
    first_grad = norm_backward(attended_grad, normed_one, inv_one, norm_gain)
    first_half = widen(first_grad.astype(jnp.bfloat16))
    output_weight_grad = tall_dot(context_flat, first_half)
    output_bias_grad = jnp.sum(first_grad, axis=0)
    context_grad = (
        wide_dot(first_half, output_weight)
        .astype(jnp.bfloat16)
        .reshape(seq_count, seq_len, local_heads, HD)
    )
    seq_index = 0
    scores = masked_scores(
        query_half[seq_index], key_half[seq_index], segment_ids[seq_index], head_scale
    )
    probs = jnp.exp(scores - total_list[seq_index])
    probs_half = probs.astype(jnp.bfloat16)
    grad_part = context_grad[seq_index]
    value_list = [
        jnp.einsum("hqk,qhd->khd", probs_half, grad_part, preferred_element_type=jnp.float32)
    ]
    prob_grad = jnp.einsum(
        "qhd,khd->hqk", grad_part, value_half[seq_index], preferred_element_type=jnp.float32
    )
    delta = jnp.einsum(
        "qhd,qhd->hq", grad_part.astype(jnp.float32), context[seq_index].astype(jnp.float32)
    )
    score_grad = (probs * (prob_grad - delta[:, :, None]) * head_scale).astype(jnp.bfloat16)
    query_list = [
        jnp.einsum(
            "hqk,khd->qhd", score_grad, key_half[seq_index], preferred_element_type=jnp.float32
        )
    ]
    key_list = [
        jnp.einsum(
            "hqk,qhd->khd", score_grad, query_half[seq_index], preferred_element_type=jnp.float32
        )
    ]
    query_grad = jnp.stack(query_list).reshape(tok_count, local_width)
    key_grad = jnp.stack(key_list).reshape(tok_count, local_width)
    value_grad = jnp.stack(value_list).reshape(tok_count, local_width)
    query_value_grad = jnp.stack([jnp.sum(query_grad, axis=0), jnp.sum(value_grad, axis=0)])
    triple_half = jnp.stack([query_grad, key_grad, value_grad], axis=1).astype(jnp.bfloat16)
    triple_grad = jnp.einsum(
        "td,tcf->dcf", gathered, triple_half, preferred_element_type=jnp.float32
    )
    input_terms = jnp.einsum(
        "tcf,dcf->td", triple_half, triple_weight, preferred_element_type=jnp.float32
    )
    input_grad = first_grad + lax.psum_scatter(
        input_terms, "tensor", scatter_dimension=1, tiled=True
    )
    (
        triple_grad,
        query_value_grad,
        output_weight_grad,
        output_bias_grad,
        norm_gain_grad,
        norm_shift_grad,
        expand_weight_grad,
        expand_bias_grad,
        reduce_weight_grad,
        reduce_bias_grad,
        final_gain_grad,
        final_shift_grad,
    ) = lax.psum(
        (
            triple_grad,
            query_value_grad,
            output_weight_grad,
            output_bias_grad,
            norm_gain_grad,
            norm_shift_grad,
            expand_weight_grad,
            expand_bias_grad,
            reduce_weight_grad,
            reduce_bias_grad,
            final_gain_grad,
            final_shift_grad,
        ),
        "dp",
    )
    return (
        layer_output,
        input_grad,
        triple_grad,
        query_value_grad,
        output_weight_grad,
        output_bias_grad,
        norm_gain_grad,
        norm_shift_grad,
        expand_weight_grad,
        expand_bias_grad,
        reduce_weight_grad,
        reduce_bias_grad,
        final_gain_grad,
        final_shift_grad,
    )


def solution(mesh):
    in_specs = (
        P("dp", "tensor"),
        P("dp", None),
        P(None, None, "tensor"),
        P(None, "tensor"),
        P("tensor", None),
        P("tensor"),
        P("tensor"),
        P("tensor"),
        P(None, "tensor"),
        P("tensor"),
        P("tensor", None),
        P("tensor"),
        P("tensor"),
        P("tensor"),
        P("dp", "tensor"),
    )
    out_specs = (
        P("dp", "tensor"),
        P("dp", "tensor"),
        P(None, None, "tensor"),
        P(None, "tensor"),
        P("tensor", None),
        P("tensor"),
        P("tensor"),
        P("tensor"),
        P(None, "tensor"),
        P("tensor"),
        P("tensor", None),
        P("tensor"),
        P("tensor"),
        P("tensor"),
    )
    return jax.shard_map(
        per_device, mesh=mesh, in_specs=in_specs, out_specs=out_specs, check_vma=False
    )
```

profile of v0, /device:TPU:0, one launch (start us, length us, event | category | flops | bytes accessed | tf_op | source)
XLA Modules:
  0.0 474.9 jit_solution(481683990149905921)
XLA Ops:
  7.2 10.4 %all_gather.12 = bf16[512,768]{0,1:T(8,128)(2,1)S(1)} all-gather(bf16[512,192]{0,1:T(8,128)(2,1)} %param.15), channel_id=1, replica_groups=mesh['dp'=8,'tensor'=4] {'tensor'}, dimensions={1}, use_global_device_ids=true | all-gather | bytes 983040 | tf_op jit(solution)/shard_map/all_gather | solution.py:23
  17.7 1.8 fusion.41
  24.3 1.6 fusion.37
  25.9 29.1 %reduce-scatter.5.cloned.1.call-done = f32[512,192]{0,1:T(8,128)} async-done(((f32[512,768]{0,1:T(8,128)}), f32[512,192]{0,1:T(8,128)}) %reduce-scatter.5.cloned.1.call-update) | async-done | bytes 393232 | tf_op jit(solution)/shard_map/reduce_scatter | solution.py:118
  56.2 5.8 %all-reduce.5 = (f32[512]{0:T(512)S(1)}, f32[512]{0:T(512)S(1)}) all-reduce(f32[512]{0:T(512)S(1)} %get-tuple-element.23, f32[512]{0:T(512)S(1)} %get-tuple-element.22), channel_id=1, replica_groups=mesh['dp'=8,'tensor'=4] {'tensor'}, use_global_device_ids=true, to_apply=%region_6.7 | all-reduce | flops 1024 | bytes 8192 | tf_op jit(solution)/shard_map/psum | solution.py:27
  62.1 8.8 %all_gather.13 = bf16[512,768]{0,1:T(8,128)(2,1)S(1)} all-gather(bf16[512,192]{0,1:T(8,128)(2,1)S(1)} %fusion.20), channel_id=1, replica_groups=mesh['dp'=8,'tensor'=4] {'tensor'}, dimensions={1}, use_global_device_ids=true | all-gather | bytes 983040 | tf_op jit(solution)/shard_map/all_gather | solution.py:23
  71.7 2.1 multiply_convert_fusion.1
  74.7 2.0 fusion.38
  76.7 28.3 %reduce-scatter.7.cloned.1.call-done = f32[512,192]{0,1:T(8,128)} async-done(((f32[512,768]{0,1:T(8,128)}), f32[512,192]{0,1:T(8,128)}) %reduce-scatter.7.cloned.1.call-update) | async-done | bytes 393232 | tf_op jit(solution)/shard_map/reduce_scatter | solution.py:131
  106.2 5.8 %all-reduce.4 = (f32[512]{0:T(512)S(1)}, f32[512]{0:T(512)S(1)}) all-reduce(f32[512]{0:T(512)S(1)} %get-tuple-element.21, f32[512]{0:T(512)S(1)} %get-tuple-element.20), channel_id=1, replica_groups=mesh['dp'=8,'tensor'=4] {'tensor'}, use_global_device_ids=true, to_apply=%region_11.12 | all-reduce | flops 1024 | bytes 8192 | tf_op jit(solution)/shard_map/psum | solution.py:27
  112.1 6.2 %all-reduce.3 = (f32[512]{0:T(512)}, f32[512]{0:T(512)S(1)}) all-reduce(f32[512]{0:T(512)S(1)} %get-tuple-element.25, f32[512]{0:T(512)S(1)} %get-tuple-element.24), channel_id=1, replica_groups=mesh['dp'=8,'tensor'=4] {'tensor'}, use_global_device_ids=true, to_apply=%region_15.16 | all-reduce | flops 1024 | bytes 8192 | tf_op jit(solution)/shard_map/psum | solution.py:27
  119.3 8.9 %all_gather.14 = bf16[512,768]{0,1:T(8,128)(2,1)S(1)} all-gather(bf16[512,192]{0,1:T(8,128)(2,1)S(1)} %fusion.28), channel_id=1, replica_groups=mesh['dp'=8,'tensor'=4] {'tensor'}, dimensions={1}, use_global_device_ids=true | all-gather | bytes 983040 | tf_op jit(solution)/shard_map/all_gather | solution.py:23
  128.2 4.3 fusion.36
  132.5 3.1 fusion.18
  135.7 28.7 %reduce-scatter.9.cloned.1.call-done = f32[512,192]{0,1:T(8,128)} async-done(((f32[512,768]{0,1:T(8,128)}), f32[512,192]{0,1:T(8,128)}) %reduce-scatter.9.cloned.1.call-update) | async-done | bytes 393232 | tf_op jit(solution)/shard_map/reduce_scatter | solution.py:151
  164.4 2.7 fusion.14
  167.1 5.7 %all-reduce.2 = (f32[512]{0:T(512)S(1)}, f32[512]{0:T(512)S(1)}) all-reduce(f32[512]{0:T(512)S(1)} %get-tuple-element.58, f32[512]{0:T(512)S(1)} %get-tuple-element.57), channel_id=1, replica_groups=mesh['dp'=8,'tensor'=4] {'tensor'}, use_global_device_ids=true, to_apply=%region_20.21 | all-reduce | flops 1024 | bytes 8192 | tf_op jit(solution)/shard_map/psum | solution.py:27
  172.9 1.4 fusion.31
  174.3 9.1 %all_gather.15 = bf16[512,768]{0,1:T(8,128)(2,1)S(1)} all-gather(bf16[512,192]{0,1:T(8,128)(2,1)S(1)} %convert_element_type.69), channel_id=1, replica_groups=mesh['dp'=8,'tensor'=4] {'tensor'}, dimensions={1}, use_global_device_ids=true | all-gather | bytes 983040 | tf_op jit(solution)/shard_map/all_gather | solution.py:23
  183.4 1.3 convolution_convert_fusion.2
  186.0 1.4 multiply_convert_fusion
  188.9 2.0 convolution_bitcast_fusion.1
  191.0 3.7 fusion.16
  194.7 2.2 fusion.40
  197.0 1.2 fusion.39
  198.2 1.9 convolution_bitcast_fusion
  200.8 37.6 %all-reduce = (f32[2,192]{1,0:T(2,128)}, f32[192]{0:T(256)}, f32[192]{0:T(256)}, f32[192]{0:T(256)}, f32[768]{0:T(1024)}, /*index=5*/f32[192]{0:T(256)}, f32[192]{0:T(256)}, f32[192]{0:T(256)}) all-reduce(f32[2,192]{1,0:T(2,128)S(1)} %pad_maximum_fusion.3, f32[192]{0:T(256)S(1)} %get-tuple-element.49, ...), channel_id=1, replica_groups=mesh['dp'=8,'tensor'=4] {'dp'}, use_global_device_ids=true, to_apply=%region_25.26 | all-reduce | flops 2304 | bytes 18432 | tf_op jit(solution)/shard_map/psum | solution.py:219
  238.4 1.8 add.169
  240.2 220.4 %all-reduce.8.cloned.1.call-done = (f32[768,3,192]{0,2,1:T(8,128)}, f32[192,768]{1,0:T(8,128)}, f32[768,768]{1,0:T(8,128)}, f32[768,768]{1,0:T(8,128)}) async-done(((f32[768,3,192]{0,2,1:T(8,128)}, f32[192,768]{1,0:T(8,128)}, f32[768,768]{1,0:T(8,128)}, f32[768,768]{1,0:T(8,128)}), (f32[768,3,192]{0,2,1:T(8,128)}, f32[192,768]{1,0:T(8,128)}, f32[768,768]{1,0:T(8,128)}, ...) | async-done | bytes 7077904 | tf_op jit(solution)/shard_map/psum | solution.py:219
  460.7 2.9 copy.50
  464.4 1.4 copy.52
  467.0 1.4 copy.53
  (155 shorter events, 15.8 us)
Async XLA Ops:
  7.2 64.5 %copy-start = (bf16[768,768]{1,0:T(8,128)(2,1)S(1)}, bf16[768,768]{1,0:T(8,128)(2,1)}, u32[]{:S(2)}) copy-start(bf16[768,768]{1,0:T(8,128)(2,1)} %param.23) | copy-start | bytes 3538948
  7.2 47.8 %reduce-scatter.5.cloned.1.call-start = ((), (), s32[]{:S(2)}) async-start(), calls=%async_computation.4 | async-start | bytes 1966080 | tf_op jit(solution)/shard_map/reduce_scatter | solution.py:118
  24.2 30.8 %copy-start.18 = (bf16[512,192]{0,1:T(8,128)(2,1)S(1)}, bf16[512,192]{0,1:T(8,128)(2,1)}, u32[]{:S(2)}) copy-start(bf16[512,192]{0,1:T(8,128)(2,1)} %param.15) | copy-start | bytes 589828
  24.3 30.8 %copy-start.50 = (f32[192]{0:T(256)S(1)}, f32[192]{0:T(256)}, u32[]{:S(2)}) copy-start(f32[192]{0:T(256)} %param.20) | copy-start | bytes 2308
  25.8 36.1 %copy-start.32 = (f32[192]{0:T(256)S(1)}, f32[192]{0:T(256)}, u32[]{:S(2)}) copy-start(f32[192]{0:T(256)} %param.21) | copy-start | bytes 2308
  25.8 36.1 %copy-start.46 = (f32[192]{0:T(256)S(1)}, f32[192]{0:T(256)}, u32[]{:S(2)}) copy-start(f32[192]{0:T(256)} %param.22) | copy-start | bytes 2308
  25.9 45.9 %copy-start.55 = (f32[768]{0:T(1024)S(1)}, f32[768]{0:T(1024)}, u32[]{:S(2)}) copy-start(f32[768]{0:T(1024)} %param.24) | copy-start | bytes 9220
  25.9 79.1 %reduce-scatter.7.cloned.1.call-start = ((), (), s32[]{:S(2)}) async-start(), calls=%async_computation.5 | async-start | bytes 1966080 | tf_op jit(solution)/shard_map/reduce_scatter | solution.py:131
  71.7 2.9 copy-start.53
  76.6 28.4 %copy-start.52 = (f32[192]{0:T(256)S(1)}, f32[192]{0:T(256)}, u32[]{:S(2)}) copy-start(f32[192]{0:T(256)} %param.26) | copy-start | bytes 2308
  76.6 35.3 %copy-start.15 = (bf16[512,192]{0,1:T(8,128)(2,1)S(1)}, bf16[512,192]{0,1:T(8,128)(2,1)}, u32[]{:S(2)}) copy-start(bf16[512,192]{0,1:T(8,128)(2,1)} %param.29) | copy-start | bytes 589828
  76.6 35.3 %copy-start.34 = (f32[192]{0:T(256)S(1)}, f32[192]{0:T(256)}, u32[]{:S(2)}) copy-start(f32[192]{0:T(256)} %param.27) | copy-start | bytes 2308
  76.7 87.7 %reduce-scatter.9.cloned.1.call-start = ((), (), s32[]{:S(2)}) async-start(), calls=%async_computation.6 | async-start | bytes 1966080 | tf_op jit(solution)/shard_map/reduce_scatter | solution.py:151
  118.4 9.8 %copy-start.54 = (bf16[768,768]{1,0:T(8,128)(2,1)S(1)}, bf16[768,768]{1,0:T(8,128)(2,1)}, u32[]{:S(2)}) copy-start(bf16[768,768]{1,0:T(8,128)(2,1)} %param.25) | copy-start | bytes 3538948
  118.4 9.8 %copy-start.30 = (f32[512]{0:T(512)}, f32[512]{0:T(512)S(1)}, u32[]{:S(2)}) copy-start(f32[512]{0:T(512)S(1)} %broadcast_multiply_fusion.1) | copy-start | bytes 6148
  128.2 4.3 copy-start.4
  135.6 28.8 %copy-start.31 = (f32[512]{0:T(512)S(1)}, f32[512]{0:T(512)}, u32[]{:S(2)}) copy-start(f32[512]{0:T(512)} %copy-done.30) | copy-start | bytes 6148
  135.6 28.8 %copy-start.33 = (f32[192]{0:T(256)S(1)}, f32[192]{0:T(256)}, u32[]{:S(2)}) copy-start(f32[192]{0:T(256)} %param.21) | copy-start | bytes 2308
  135.6 28.8 %copy-start.35 = (f32[192]{0:T(256)S(1)}, f32[192]{0:T(256)}, u32[]{:S(2)}) copy-start(f32[192]{0:T(256)} %param.27) | copy-start | bytes 2308
  135.6 28.8 %copy-start.39 = (f32[512]{0:T(512)S(1)}, f32[512]{0:T(512)}, u32[]{:S(2)}) copy-start(f32[512]{0:T(512)} %get-tuple-element.43) | copy-start | bytes 6148
  135.6 28.8 %copy-start.51 = (f32[192]{0:T(256)S(1)}, f32[192]{0:T(256)}, u32[]{:S(2)}) copy-start(f32[192]{0:T(256)} %param.28) | copy-start | bytes 2308
  135.6 102.8 %reduce-scatter.11.cloned.1.call-start = ((), (), s32[]{:S(2)}) async-start(), calls=%async_computation.7 | async-start | bytes 1966080 | tf_op jit(solution)/shard_map/reduce_scatter | solution.py:203
  172.9 11.8 %copy-start.2 = (f32[3,512,512]{1,2,0:T(8,128)S(1)}, f32[3,512,512]{1,2,0:T(8,128)}, u32[]{:S(2)}) copy-start(f32[3,512,512]{1,2,0:T(8,128)} %copy-done.1) | copy-start | bytes 9437188
  174.3 10.4 %copy-start.9 = (pred[512,512]{0,1:T(8,128)(4,1)S(1)}, pred[512,512]{0,1:T(8,128)(4,1)}, u32[]{:S(2)}) copy-start(pred[512,512]{0,1:T(8,128)(4,1)} %copy-done.8) | copy-start | bytes 786436
  174.3 10.4 %copy-start.38 = (f32[3,512]{1,0:T(4,128)S(1)}, f32[3,512]{1,0:T(4,128)}, u32[]{:S(2)}) copy-start(f32[3,512]{1,0:T(4,128)} %copy-done.37) | copy-start | bytes 18436
  185.8 2.9 copy-start.56
  191.0 269.7 %all-reduce.8.cloned.1.call-start = ((), (), s32[]{:S(2)}) async-start(), calls=%async_computation.8 | async-start | bytes 14155776 | tf_op jit(solution)/shard_map/psum | solution.py:219
  191.0 3.7 copy-start.5
  191.0 3.7 copy-start.20
  460.7 3.0 copy-start.21
  460.7 3.8 copy-start.7
  464.4 2.5 copy-start.6
  (31 other events, 37.6 us)
Sparse Core Ops, SparseCore 0:
  26.0 29.0 reduce-scatter.4
  76.8 28.1 reduce-scatter.6
  135.7 28.6 reduce-scatter.8
  191.1 28.1 reduce-scatter.10
  224.7 235.8 all-reduce.7
where the time goes:
time: 476 us; the launch traced here: 475 us
  waiting for transfers between devices  307 us (64%)
  blocking collectives  98.2 us (21%)
  matrix products  32.3 us (7%)
  between operations  14.3 us (3%)
  local copies, waits for them, and re-layouts  12.8 us (3%)
  other arithmetic  10.5 us (2%)
    psum x1, waiting for transfers between devices, per_device(): lax.psum((triple_grad, query_value_grad, output_weight_grad, output_bias_...  220 us
    psum x1, blocking collectives, per_device(): lax.psum((triple_grad, query_value_grad, output_weight_grad, output_bias_...  37.6 us
    all_gather x4, blocking collectives, widen(): return lax.all_gather(piece, 'tensor', axis=1, tiled=True)  37.1 us
    reduce_scatter x1, waiting for transfers between devices, per_device(): lax.psum_scatter(jnp.dot(context_flat, output_weight, preferred_element_t...  29.1 us
    reduce_scatter x1, waiting for transfers between devices, per_device(): lax.psum_scatter(wide_dot(act_half, expand_weight), 'tensor', scatter_dim...  28.7 us
    reduce_scatter x1, waiting for transfers between devices, per_device(): lax.psum_scatter(jnp.dot(activated, reduce_weight, preferred_element_type...  28.3 us
    psum x4, blocking collectives, row_stats(): return lax.psum((jnp.sum(first, axis=1), jnp.sum(second, axis=1)), 'tensor')  23.5 us
    unnamed x120, local copies, waits for them, and re-layouts  11.6 us
  transfers between devices with their start and end apart: 5, of which 4 were waited for; matrix products, arithmetic and copies ran while one was open for 2% of the time, Pallas kernels for 0%

commit v1 on v0

--- a/solution.py
+++ b/solution.py
@@ -8,6 +8,27 @@
 EPS = 1e-06
 
 
+def gather_around(x, axis, dim):
+    length, index, rows = (lax.axis_size(axis), lax.axis_index(axis), x.shape[dim])
+    right = [(i, (i + 1) % length) for i in range(length)]
+    backward = [(i, (i - 1) % length) for i in range(length)]
+    out = jnp.zeros((*x.shape[:dim], length * rows, *x.shape[dim + 1 :]), x.dtype)
+    out = lax.dynamic_update_slice_in_dim(out, x, index * rows, axis=dim)
+    from_left = from_right = x
+    halfway = length // 2
+    for step in range(1, halfway + 1):
+        from_left = lax.ppermute(from_left, axis, right)
+        out = lax.dynamic_update_slice_in_dim(
+            out, from_left, (index - step) % length * rows, axis=dim
+        )
+        if step < length - halfway:
+            from_right = lax.ppermute(from_right, axis, backward)
+            out = lax.dynamic_update_slice_in_dim(
+                out, from_right, (index + step) % length * rows, axis=dim
+            )
+    return out
+
+
 def gelu_value(pre_act):
     return 0.5 * pre_act * (1.0 + lax.erf(pre_act * 0.7071067811865476))
 
@@ -20,7 +41,7 @@
 
 
 def widen(piece):
-    return lax.all_gather(piece, "tensor", axis=1, tiled=True)
+    return gather_around(piece, "tensor", 1)
 
 
 def row_stats(first, second):

time: 476 us -> 549 us (1.15)
  local copies, waits for them, and re-layouts: 12.8 us -> 86.8 us
  blocking collectives: 98.2 us -> 61.4 us
  waiting for transfers between devices: 307 us -> 325 us
  starting transfers between devices: 0.2 us -> 11.6 us
  other arithmetic: 10.5 us -> 16.2 us
    dynamic_update_slice x0 -> x16, local copies, waits for them, and re-layouts: none -> 48.5 us  [the longest x8 21.7 us: gather_around(): lax.dynamic_update_slice_in_dim(out, from_left, (index - step) % length *...]
    all_gather x4 -> x0, blocking collectives: 37.1 us -> none  [widen(): return lax.all_gather(piece, 'tensor', axis=1, tiled=True)]
    ppermute x0 -> x12, local copies, waits for them, and re-layouts: none -> 17.1 us  [the longest x8 11.4 us: gather_around(): from_left = lax.ppermute(from_left, axis, right)]
    ppermute x0 -> x12, starting transfers between devices: none -> 11.4 us  [the longest x4 7.25 us: gather_around(): from_right = lax.ppermute(from_right, axis, backward)]
    ppermute x0 -> x12, waiting for transfers between devices: none -> 11.2 us  [the longest x8 11.2 us: gather_around(): from_left = lax.ppermute(from_left, axis, right)]
    unnamed x120 -> x109, local copies, waits for them, and re-layouts: 11.6 us -> 14.4 us
  transfers between devices with their start and end apart: 5 -> 17, of which waited for: 4 -> 7; matrix products, arithmetic and copies ran while one was open for 2% -> 13% of each run, Pallas kernels for 0% -> 0%
where the time goes in v1:
time: 549 us; the launch traced here: 547 us
  waiting for transfers between devices  325 us (59%)
  local copies, waits for them, and re-layouts  86.8 us (16%)
  blocking collectives  61.4 us (11%)
  matrix products  31.1 us (6%)
  other arithmetic  16.2 us (3%)
  between operations  14.6 us (3%)
  starting transfers between devices  11.6 us (2%)
    psum x1, waiting for transfers between devices, per_device(): lax.psum((triple_grad, query_value_grad, output_weight_grad, output_bias_...  223 us
    psum x1, blocking collectives, per_device(): lax.psum((triple_grad, query_value_grad, output_weight_grad, output_bias_...  37 us
    reduce_scatter x1, waiting for transfers between devices, per_device(): lax.psum_scatter(wide_dot(act_half, expand_weight), 'tensor', scatter_dim...  30.4 us
    reduce_scatter x1, waiting for transfers between devices, per_device(): lax.psum_scatter(jnp.dot(activated, reduce_weight, preferred_element_type...  30.3 us
    reduce_scatter x1, waiting for transfers between devices, per_device(): lax.psum_scatter(jnp.dot(context_flat, output_weight, preferred_element_t...  29.9 us
    psum x4, blocking collectives, row_stats(): return lax.psum((jnp.sum(first, axis=1), jnp.sum(second, axis=1)), 'tensor')  24.4 us
    dynamic_update_slice x8, local copies, waits for them, and re-layouts, gather_around(): lax.dynamic_update_slice_in_dim(out, from_left, (index - step) % length *...  21.7 us
    dynamic_update_slice x4, local copies, waits for them, and re-layouts, gather_around(): lax.dynamic_update_slice_in_dim(out, from_right, (index + step) % length...  14.5 us
  transfers between devices with their start and end apart: 17, of which 7 were waited for; matrix products, arithmetic and copies ran while one was open for 13% of the time, Pallas kernels for 0%

profile of v1, /device:TPU:0, one launch (start us, length us, event | category | flops | bytes accessed | tf_op | source)
XLA Modules:
  0.0 547.0 jit_solution(9334502444410470658)
XLA Ops:
  11.9 2.6 dynamic_update_slice.48
  17.4 2.4 dynamic_update_slice.49
  20.8 3.3 dynamic_update_slice.50
  33.6 29.9 %reduce-scatter.5.cloned.1.call-done = f32[512,192]{0,1:T(8,128)} async-done(((f32[512,768]{0,1:T(8,128)}), f32[512,192]{0,1:T(8,128)}) %reduce-scatter.5.cloned.1.call-update) | async-done | bytes 393232 | tf_op jit(solution)/shard_map/reduce_scatter | solution.py:139
  64.6 5.8 %all-reduce.5 = (f32[512]{0:T(512)S(1)}, f32[512]{0:T(512)S(1)}) all-reduce(f32[512]{0:T(512)S(1)} %get-tuple-element.23, f32[512]{0:T(512)S(1)} %get-tuple-element.22), channel_id=1, replica_groups=mesh['dp'=8,'tensor'=4] {'tensor'}, use_global_device_ids=true, to_apply=%region_6.7 | all-reduce | flops 1024 | bytes 8192 | tf_op jit(solution)/shard_map/psum | solution.py:48
  73.0 3.8 collective-permute-done.3
  78.5 2.6 dynamic_update_slice.52
  82.2 2.4 dynamic_update_slice.53
  85.7 3.3 dynamic_update_slice.54
  96.8 30.3 %reduce-scatter.7.cloned.1.call-done = f32[512,192]{0,1:T(8,128)} async-done(((f32[512,768]{0,1:T(8,128)}), f32[512,192]{0,1:T(8,128)}) %reduce-scatter.7.cloned.1.call-update) | async-done | bytes 393232 | tf_op jit(solution)/shard_map/reduce_scatter | solution.py:152
  128.9 6.4 %all-reduce.4 = (f32[512]{0:T(512)}, f32[512]{0:T(512)}) all-reduce(f32[512]{0:T(512)} %get-tuple-element.21, f32[512]{0:T(512)S(1)} %get-tuple-element.20), channel_id=1, replica_groups=mesh['dp'=8,'tensor'=4] {'tensor'}, use_global_device_ids=true, to_apply=%region_11.12 | all-reduce | flops 1024 | bytes 8192 | tf_op jit(solution)/shard_map/psum | solution.py:48
  137.7 6.3 %all-reduce.3 = (f32[512]{0:T(512)}, f32[512]{0:T(512)}) all-reduce(f32[512]{0:T(512)} %get-tuple-element.25, f32[512]{0:T(512)} %get-tuple-element.24), channel_id=1, replica_groups=mesh['dp'=8,'tensor'=4] {'tensor'}, use_global_device_ids=true, to_apply=%region_15.16 | all-reduce | flops 1024 | bytes 8192 | tf_op jit(solution)/shard_map/psum | solution.py:48
  148.8 3.7 collective-permute-done.6
  156.2 3.4 dynamic_update_slice.56
  161.4 3.2 dynamic_update_slice.57
  166.4 3.8 dynamic_update_slice.58
  172.0 3.4 dynamic_update_slice.59
  175.4 3.7 fusion.33
  182.0 30.4 %reduce-scatter.9.cloned.1.call-done = f32[512,192]{0,1:T(8,128)} async-done(((f32[512,768]{0,1:T(8,128)}), f32[512,192]{0,1:T(8,128)}) %reduce-scatter.9.cloned.1.call-update) | async-done | bytes 393232 | tf_op jit(solution)/shard_map/reduce_scatter | solution.py:172
  212.4 2.8 fusion.13
  215.2 5.9 %all-reduce.2 = (f32[512]{0:T(512)S(1)}, f32[512]{0:T(512)S(1)}) all-reduce(f32[512]{0:T(512)} %get-tuple-element.58, f32[512]{0:T(512)} %get-tuple-element.57), channel_id=1, replica_groups=mesh['dp'=8,'tensor'=4] {'tensor'}, use_global_device_ids=true, to_apply=%region_20.21 | all-reduce | flops 1024 | bytes 8192 | tf_op jit(solution)/shard_map/psum | solution.py:48
  224.8 3.8 collective-permute-done.9
  231.1 3.6 dynamic_update_slice.60
  236.5 3.6 dynamic_update_slice.61
  241.9 4.1 dynamic_update_slice.62
  247.8 3.1 dynamic_update_slice.63
  252.4 3.1 fusion.32
  261.2 3.5 fusion.15
  264.7 2.2 fusion.38
  270.7 37.0 %all-reduce = (f32[2,192]{1,0:T(2,128)}, f32[192]{0:T(256)}, f32[192]{0:T(256)}, f32[192]{0:T(256)}, f32[768]{0:T(1024)}, /*index=5*/f32[192]{0:T(256)}, f32[192]{0:T(256)}, f32[192]{0:T(256)}) all-reduce(f32[2,192]{1,0:T(2,128)S(1)} %pad_maximum_fusion.1, f32[192]{0:T(256)S(1)} %get-tuple-element.49, ...), channel_id=1, replica_groups=mesh['dp'=8,'tensor'=4] {'dp'}, use_global_device_ids=true, to_apply=%region_25.26 | all-reduce | flops 2304 | bytes 18432 | tf_op jit(solution)/shard_map/psum | solution.py:240
  309.6 223.2 %all-reduce.8.cloned.1.call-done = (f32[768,3,192]{0,2,1:T(8,128)}, f32[192,768]{1,0:T(8,128)}, f32[768,768]{1,0:T(8,128)}, f32[768,768]{1,0:T(8,128)}) async-done(((f32[768,3,192]{0,2,1:T(8,128)}, f32[192,768]{1,0:T(8,128)}, f32[768,768]{1,0:T(8,128)}, f32[768,768]{1,0:T(8,128)}), (f32[768,3,192]{0,2,1:T(8,128)}, f32[192,768]{1,0:T(8,128)}, f32[768,768]{1,0:T(8,128)}, ...) | async-done | bytes 7077904 | tf_op jit(solution)/shard_map/psum | solution.py:240
  532.8 2.9 copy.82
  (200 shorter events, 82.8 us)
Async XLA Ops:
  7.2 84.7 %copy-start = (bf16[768,768]{1,0:T(8,128)(2,1)S(1)}, bf16[768,768]{1,0:T(8,128)(2,1)}, u32[]{:S(2)}) copy-start(bf16[768,768]{1,0:T(8,128)(2,1)} %param.23) | copy-start | bytes 3538948
  7.2 8.7 %copy-start.37 = (s32[1,512]{1,0:T(1,128)S(1)}, s32[1,512]{1,0:T(1,128)}, u32[]{:S(2)}) copy-start(s32[1,512]{1,0:T(1,128)} %param.16) | copy-start | bytes 6148
  7.2 56.3 %reduce-scatter.5.cloned.1.call-start = ((), (), s32[]{:S(2)}) async-start(), calls=%async_computation.4 | async-start | bytes 1966080 | tf_op jit(solution)/shard_map/reduce_scatter | solution.py:139
  7.2 7.3 %collective-permute-start = (bf16[512,192]{0,1:T(8,128)(2,1)}, bf16[512,192]{0,1:T(8,128)(2,1)}, u32[]{:S(2)}, u32[]{:S(2)}) collective-permute-start(bf16[512,192]{0,1:T(8,128)(2,1)} %param.15), channel_id=1, source_target_pairs={{0,1},{1,2},{2,3},{3,0},{4,5},{5,6},{6,7},{7,4},{8,9},{9,10},{10,1... | collective-permute-start | bytes 589832 | tf_op jit(solution)/shard_map/ppermute | solution.py:20
  7.8 12.0 %collective-permute-start.1 = (bf16[512,192]{0,1:T(8,128)(2,1)}, bf16[512,192]{0,1:T(8,128)(2,1)}, u32[]{:S(2)}, u32[]{:S(2)}) collective-permute-start(bf16[512,192]{0,1:T(8,128)(2,1)} %param.15), channel_id=1, source_target_pairs={{0,3},{1,0},{2,1},{3,2},{4,7},{5,4},{6,5},{7,6},{8,11},{9,8},{10,9... | collective-permute-start | bytes 589832 | tf_op jit(solution)/shard_map/ppermute | solution.py:25
  11.8 17.6 %copy-start.47 = (f32[3,64]{1,0:T(4,128)}, f32[3,64]{1,0:T(4,128)S(1)}, u32[]{:S(2)}) copy-start(f32[3,64]{1,0:T(4,128)S(1)} %add.204) | copy-start | bytes 2308
  11.9 15.9 %copy-start.33 = (f32[3,64]{1,0:T(4,128)}, f32[3,64]{1,0:T(4,128)S(1)}, u32[]{:S(2)}) copy-start(f32[3,64]{1,0:T(4,128)S(1)} %add.207) | copy-start | bytes 2308
  14.6 9.6 %collective-permute-start.2 = (bf16[512,192]{0,1:T(8,128)(2,1)}, bf16[512,192]{0,1:T(8,128)(2,1)}, u32[]{:S(2)}, u32[]{:S(2)}) collective-permute-start(bf16[512,192]{0,1:T(8,128)(2,1)} %collective-permute-done), channel_id=1, source_target_pairs={{0,1},{1,2},{2,3},{3,0},{4,5},{5,6},{6,7},{7,4},{8,9},{9,10},{10,1... | collective-permute-start | bytes 589832 | tf_op jit(solution)/shard_map/ppermute | solution.py:20
  15.9 11.1 %copy-start.20 = (bf16[768,3,192]{0,2,1:T(8,128)(2,1)S(1)}, bf16[768,3,192]{0,2,1:T(8,128)(2,1)}, u32[]{:S(2)}) copy-start(bf16[768,3,192]{0,2,1:T(8,128)(2,1)} %param.17) | copy-start | bytes 2654212
  16.2 13.2 %copy-start.10 = (pred[512,512]{0,1:T(8,128)(4,1)}, pred[512,512]{0,1:T(8,128)(4,1)S(1)}, u32[]{:S(2)}) copy-start(pred[512,512]{0,1:T(8,128)(4,1)S(1)} %broadcast_compare_fusion) | copy-start | bytes 786436
  31.9 31.6 %copy-start.26 = (bf16[512,192]{0,1:T(8,128)(2,1)S(1)}, bf16[512,192]{0,1:T(8,128)(2,1)}, u32[]{:S(2)}) copy-start(bf16[512,192]{0,1:T(8,128)(2,1)} %param.15) | copy-start | bytes 589828
  31.9 31.6 %copy-start.49 = (f32[192]{0:T(256)S(1)}, f32[192]{0:T(256)}, u32[]{:S(2)}) copy-start(f32[192]{0:T(256)} %param.20) | copy-start | bytes 2308
  33.5 36.9 %copy-start.36 = (f32[192]{0:T(256)S(1)}, f32[192]{0:T(256)}, u32[]{:S(2)}) copy-start(f32[192]{0:T(256)} %param.21) | copy-start | bytes 2308
  33.5 36.9 %copy-start.46 = (f32[192]{0:T(256)S(1)}, f32[192]{0:T(256)}, u32[]{:S(2)}) copy-start(f32[192]{0:T(256)} %param.22) | copy-start | bytes 2308
  33.5 93.6 %reduce-scatter.7.cloned.1.call-start = ((), (), s32[]{:S(2)}) async-start(), calls=%async_computation.5 | async-start | bytes 1966080 | tf_op jit(solution)/shard_map/reduce_scatter | solution.py:152
  71.2 5.5 %collective-permute-start.3 = (bf16[512,192]{0,1:T(8,128)(2,1)}, bf16[512,192]{0,1:T(8,128)(2,1)}, u32[]{:S(2)}, u32[]{:S(2)}) collective-permute-start(bf16[512,192]{0,1:T(8,128)(2,1)} %fusion.19), channel_id=1, source_target_pairs={{0,1},{1,2},{2,3},{3,0},{4,5},{5,6},{6,7},{7,4},{8,9},{9,10},{10,1... | collective-permute-start | bytes 589832 | tf_op jit(solution)/shard_map/ppermute | solution.py:20
  71.2 13.4 %collective-permute-start.4 = (bf16[512,192]{0,1:T(8,128)(2,1)}, bf16[512,192]{0,1:T(8,128)(2,1)}, u32[]{:S(2)}, u32[]{:S(2)}) collective-permute-start(bf16[512,192]{0,1:T(8,128)(2,1)} %fusion.19), channel_id=1, source_target_pairs={{0,3},{1,0},{2,1},{3,2},{4,7},{5,4},{6,5},{7,6},{8,11},{9,8},{10,9... | collective-permute-start | bytes 589832 | tf_op jit(solution)/shard_map/ppermute | solution.py:25
  76.8 12.2 %collective-permute-start.5 = (bf16[512,192]{0,1:T(8,128)(2,1)}, bf16[512,192]{0,1:T(8,128)(2,1)}, u32[]{:S(2)}, u32[]{:S(2)}) collective-permute-start(bf16[512,192]{0,1:T(8,128)(2,1)} %collective-permute-done.3), channel_id=1, source_target_pairs={{0,1},{1,2},{2,3},{3,0},{4,5},{5,6},{6,7},{7,4},{8,9},{9,10},{10,1... | collective-permute-start | bytes 589832 | tf_op jit(solution)/shard_map/ppermute | solution.py:20
  81.1 10.7 %copy-start.51 = (f32[768]{0:T(1024)S(1)}, f32[768]{0:T(1024)}, u32[]{:S(2)}) copy-start(f32[768]{0:T(1024)} %param.24) | copy-start | bytes 9220
  96.8 115.6 %reduce-scatter.9.cloned.1.call-start = ((), (), s32[]{:S(2)}) async-start(), calls=%async_computation.6 | async-start | bytes 1966080 | tf_op jit(solution)/shard_map/reduce_scatter | solution.py:172
  147.0 5.4 collective-permute-start.6
  147.1 17.6 %collective-permute-start.7 = (bf16[512,192]{0,1:T(8,128)(2,1)}, bf16[512,192]{0,1:T(8,128)(2,1)}, u32[]{:S(2)}, u32[]{:S(2)}) collective-permute-start(bf16[512,192]{0,1:T(8,128)(2,1)} %fusion.25), channel_id=1, source_target_pairs={{0,3},{1,0},{2,1},{3,2},{4,7},{5,4},{6,5},{7,6},{8,11},{9,8},{10,9... | collective-permute-start | bytes 589832 | tf_op jit(solution)/shard_map/ppermute | solution.py:25
  152.5 17.8 %collective-permute-start.8 = (bf16[512,192]{0,1:T(8,128)(2,1)}, bf16[512,192]{0,1:T(8,128)(2,1)}, u32[]{:S(2)}, u32[]{:S(2)}) collective-permute-start(bf16[512,192]{0,1:T(8,128)(2,1)} %collective-permute-done.6), channel_id=1, source_target_pairs={{0,1},{1,2},{2,3},{3,0},{4,5},{5,6},{6,7},{7,4},{8,9},{9,10},{10,1... | collective-permute-start | bytes 589832 | tf_op jit(solution)/shard_map/ppermute | solution.py:20
  181.9 125.8 %reduce-scatter.11.cloned.1.call-start = ((), (), s32[]{:S(2)}) async-start(), calls=%async_computation.7 | async-start | bytes 1966080 | tf_op jit(solution)/shard_map/reduce_scatter | solution.py:224
  222.3 6.9 %copy-start.5 = (f32[512,192]{0,1:T(8,128)}, f32[512,192]{0,1:T(8,128)S(1)}, u32[]{:S(2)}) copy-start(f32[512,192]{0,1:T(8,128)S(1)} %get-tuple-element.50) | copy-start | bytes 1179652
  223.1 5.5 %collective-permute-start.9 = (bf16[512,192]{0,1:T(8,128)(2,1)}, bf16[512,192]{0,1:T(8,128)(2,1)}, u32[]{:S(2)}, u32[]{:S(2)}) collective-permute-start(bf16[512,192]{0,1:T(8,128)(2,1)} %convert_element_type.69), channel_id=1, source_target_pairs={{0,1},{1,2},{2,3},{3,0},{4,5},{5,6},{6,7},{7,4},{8,9},{9,10},{10,1... | collective-permute-start | bytes 589832 | tf_op jit(solution)/shard_map/ppermute | solution.py:20
  223.1 17.0 %collective-permute-start.10 = (bf16[512,192]{0,1:T(8,128)(2,1)}, bf16[512,192]{0,1:T(8,128)(2,1)}, u32[]{:S(2)}, u32[]{:S(2)}) collective-permute-start(bf16[512,192]{0,1:T(8,128)(2,1)} %convert_element_type.69), channel_id=1, source_target_pairs={{0,3},{1,0},{2,1},{3,2},{4,7},{5,4},{6,5},{7,6},{8,11},{9,8},{10,9... | collective-permute-start | bytes 589832 | tf_op jit(solution)/shard_map/ppermute | solution.py:25
  228.6 17.4 %collective-permute-start.11 = (bf16[512,192]{0,1:T(8,128)(2,1)}, bf16[512,192]{0,1:T(8,128)(2,1)}, u32[]{:S(2)}, u32[]{:S(2)}) collective-permute-start(bf16[512,192]{0,1:T(8,128)(2,1)} %collective-permute-done.9), channel_id=1, source_target_pairs={{0,1},{1,2},{2,3},{3,0},{4,5},{5,6},{6,7},{7,4},{8,9},{9,10},{10,1... | collective-permute-start | bytes 589832 | tf_op jit(solution)/shard_map/ppermute | solution.py:20
  240.1 12.2 %copy-start.39 = (f32[3,512]{1,0:T(4,128)S(1)}, f32[3,512]{1,0:T(4,128)}, u32[]{:S(2)}) copy-start(f32[3,512]{1,0:T(4,128)} %copy-done.38) | copy-start | bytes 18436
  261.1 271.7 %all-reduce.8.cloned.1.call-start = ((), (), s32[]{:S(2)}) async-start(), calls=%async_computation.8 | async-start | bytes 14155776 | tf_op jit(solution)/shard_map/psum | solution.py:240
  270.0 37.8 %copy-start.6 = (f32[512,192]{0,1:T(8,128)S(1)}, f32[512,192]{0,1:T(8,128)}, u32[]{:S(2)}) copy-start(f32[512,192]{0,1:T(8,128)} %copy-done.5) | copy-start | bytes 1179652
  532.8 3.8 copy-start.9
  (37 other events, 66.5 us)
Sparse Core Ops, SparseCore 0:
  33.7 29.7 reduce-scatter.4
  96.9 30.1 reduce-scatter.6
  182.0 30.2 reduce-scatter.8
  261.2 30.1 reduce-scatter.10
  296.8 235.8 all-reduce.7
